TPU v7x, 32 devices: a whole 2x2x4 slice. The times are simulated.
32 devices in a mesh: band: 4 (over y, x), pw: 8 (over z, core).
Axes of the slice: x: 2, y: 2, z: 4, core: 2. Of those that a mesh axis runs over, the one named last changes fastest.
Arguments:
- psi: float32 [2, 8, 16384], P(None, None, 'pw'), may hold values from -60 to 60
- energies: float32 [8], P('band'), may hold values from -2 to 0
- kinetic: float32 [16384], P('pw'), may hold values from 0.05 to 20
- vloc: float32 [128, 128, 128], P('pw'), may hold values from 0.5 to 2
- dv: float32 [128, 128, 128], P('pw'), may hold values from -5 to 5
- beta: float32 [2, 64, 16384], P(None, None, 'pw'), may hold values from -0.046875 to 0.046875
- nl_diag: float32 [64], replicated, may hold values from 1 to 10
- nl_coupling: float32 [64], replicated, may hold values from -4 to 4
- proj_counts: int32 [16], replicated, may hold values from 1 to 13, 64 in all
- pw_map: int32 [16384], P('pw'), may hold values from 0 to 16383, as said below
- stick_pos: int32 [1024], replicated, may hold values from 0 to 16383, as said below
Outputs:
- dpsi: float32 [2, 8, 16384], P(None, 'band', 'pw')
- residual: float32 [2, 8, 16384], P(None, 'band', 'pw')
- drho: float32 [128, 128, 128], P('pw', 'band')
Inputs may be any that keep to these rules, and one draw needn't show every extreme that they name: `pw_map`: within each block of 2048 entries (the plane waves of one pw index) the values are distinct, and each block holds 0 and 16383. `stick_pos`: all values distinct; 0 and 16383 appear.
All inputs are finite; a program needn't handle non-finite values.
Results may differ from a plain program's by a relative error of at most 0.0003.
Values sent between devices are 32-bit elements; how exact they have to be, the bound alone decides.
A program may use at most 256 MiB of HBM per device.

v0:
```python
import math
import jax
import jax.numpy as jnp
from jax import lax
from jax.sharding import PartitionSpec as P

ITERS = 2
PRECISE = lax.Precision.HIGHEST
ALPHA_SHIFT = 4.0


def dft_tables(length):
    positions = jnp.arange(length, dtype=jnp.int32)
    phases = positions[:, None] * positions[None, :] % length
    angles = phases.astype(jnp.float32) * (2.0 * math.pi / length)
    return (jnp.cos(angles), jnp.sin(angles))


def complex_transform(values_in, tables, direction_sign, einsum_form):
    cosine_table, sine_table = tables
    real_part, imag_part = (values_in[0], values_in[1])

    def product(table, operand):
        return jnp.einsum(einsum_form, table, operand, precision=PRECISE)

    return jnp.stack(
        [
            product(cosine_table, real_part) - direction_sign * product(sine_table, imag_part),
            product(cosine_table, imag_part) + direction_sign * product(sine_table, real_part),
        ]
    )


def project_onto(basis, vector):

    def product(left, right):
        return jnp.einsum("kg,ng->kn", left, right, precision=PRECISE)

    return jnp.stack(
        [
            product(basis[0], vector[0]) + product(basis[1], vector[1]),
            product(basis[0], vector[1]) - product(basis[1], vector[0]),
        ]
    )


def expand(basis, weights):

    def product(left, right):
        return jnp.einsum("kn,kg->ng", left, right, precision=PRECISE)

    return jnp.stack(
        [
            product(weights[0], basis[0]) - product(weights[1], basis[1]),
            product(weights[0], basis[1]) + product(weights[1], basis[0]),
        ]
    )


def dot_bands(left, right):
    return jnp.sum(left * right, axis=(0, 2))


def shards(
    psi, energies, kinetic, vloc, dv, beta, nl_diag, nl_coupling, proj_counts, pw_map, stick_pos
):
    grid_size = vloc.shape[1]
    plane_count = vloc.shape[0]
    columns = stick_pos.shape[0] // lax.axis_size("pw")
    total_pw = kinetic.shape[0] * lax.axis_size("pw")
    block_bands = energies.shape[0]
    norm_scale = 1.0 / math.sqrt(grid_size**3)
    tables = dft_tables(grid_size)
    own_states = lax.dynamic_slice_in_dim(psi, lax.axis_index("band") * block_bands, block_bands, 1)
    block_ends = jnp.cumsum(proj_counts)
    proj_index = jnp.arange(beta.shape[1], dtype=jnp.int32)
    atom_of = jnp.sum((proj_index[:, None] >= block_ends[None, :]).astype(jnp.int32), axis=1)
    same_atom = (atom_of[:, None] == atom_of[None, :]).astype(jnp.float32)

    def to_sticks(coeffs):
        item_count = coeffs.shape[1]
        flat_grid = (
            jnp.zeros((2, item_count, grid_size * columns), jnp.float32)
            .at[:, :, pw_map]
            .set(coeffs)
        )
        sticks = flat_grid.reshape(2, item_count, grid_size, columns)
        return complex_transform(sticks, tables, 1.0, "zk,bks->bzs")

    def planes_inverse(received):
        item_count = received.shape[1]
        flat_grid = jnp.zeros((2, item_count, plane_count, grid_size * grid_size), jnp.float32)
        flat_grid = flat_grid.at[:, :, :, stick_pos].set(received)
        field = flat_grid.reshape(2, item_count, plane_count, grid_size, grid_size)
        field = complex_transform(field, tables, 1.0, "yk,bpkx->bpyx")
        field = complex_transform(field, tables, 1.0, "xk,bpyk->bpyx")
        return field * norm_scale

    def planes_forward(field):
        item_count = field.shape[1]
        spectrum = complex_transform(field, tables, -1.0, "yk,bpkx->bpyx")
        spectrum = complex_transform(spectrum, tables, -1.0, "xk,bpyk->bpyx")
        spectrum = spectrum.reshape(2, item_count, plane_count, grid_size * grid_size)
        return jnp.take(spectrum, stick_pos, axis=3)

    def with_potential(potential):

        def apply_field(received):
            field = planes_inverse(received)
            return (field, planes_forward(field * potential))

        return apply_field

    def real_space(coeffs, plane_fn):
        return plane_fn(
            lax.all_to_all(to_sticks(coeffs), "pw", split_axis=2, concat_axis=3, tiled=True)
        )

    def from_sticks(back_values):
        sticks = lax.all_to_all(back_values, "pw", split_axis=3, concat_axis=2, tiled=True)
        item_count = sticks.shape[1]
        spectrum = complex_transform(sticks, tables, -1.0, "zk,bks->bzs") * norm_scale
        spectrum = spectrum.reshape(2, item_count, grid_size * columns)
        return jnp.take(spectrum, pw_map, axis=2)

    def projections(vector):
        return lax.psum((project_onto(psi, vector), project_onto(beta, vector)), "pw")

    def preconditioned_norm(residual, precond_res):
        return lax.psum(dot_bands(residual, precond_res), "pw")

    diagonal_shift = kinetic[None, None, :] - energies[None, :, None]
    precond = 1.0 / (1.0 + diagonal_shift)
    state_planes, dv_back = real_space(own_states, with_potential(dv))
    dvpsi = from_sticks(dv_back)
    rhs_state, rhs_beta = projections(dvpsi)
    rhs = -(dvpsi - expand(psi, rhs_state) / total_pw)
    solution = jnp.zeros_like(rhs)
    residual = rhs
    search = precond * residual
    norm_now = preconditioned_norm(residual, search)
    for iteration in range(ITERS):
        search_planes, local_back = real_space(search, with_potential(vloc))
        local_part = from_sticks(local_back)
        state_proj, beta_proj = projections(search)
        weighted = nl_coupling[None, :, None] * beta_proj
        grouped = jnp.einsum("ij,cjn->cin", same_atom, weighted, precision=PRECISE)
        nonlocal_part = expand(
            beta, nl_diag[None, :, None] * beta_proj + nl_coupling[None, :, None] * grouped
        )
        occupied_part = ALPHA_SHIFT / total_pw * expand(psi, state_proj)
        image = diagonal_shift * search + local_part + nonlocal_part + occupied_part
        step_len = norm_now / lax.psum(dot_bands(search, image), "pw")
        solution = solution + step_len[None, :, None] * search
        residual = residual - step_len[None, :, None] * image
        if iteration + 1 < ITERS:
            precond_res = precond * residual
            norm_next = preconditioned_norm(residual, precond_res)
            ratio = norm_next / norm_now
            search = precond_res + ratio[None, :, None] * search
            norm_now = norm_next
    solution_planes = real_space(solution, planes_inverse)
    density_scale = 2.0 * grid_size**3 / total_pw
    density_term = density_scale * jnp.sum(state_planes * solution_planes, axis=(0, 1))
    drho = lax.psum_scatter(density_term, "band", scatter_dimension=1, tiled=True)
    return (solution, residual, drho)


def solution(mesh):
    placed = (
        P(None, None, "pw"),
        P("band"),
        P("pw"),
        P("pw", None, None),
        P("pw", None, None),
        P(None, None, "pw"),
        P(),
        P(),
        P(),
        P("pw"),
        P(),
    )
    return jax.shard_map(
        shards,
        mesh=mesh,
        in_specs=placed,
        out_specs=(P(None, "band", "pw"), P(None, "band", "pw"), P("pw", "band", None)),
        check_vma=False,
    )
```

profile of v0, /device:TPU:0, one launch (start us, length us, event | category | flops | bytes accessed | tf_op | source)
XLA Modules:
  0.0 2317.2 jit_solution(12426958503764950152)
XLA Ops:
  15.2 186.4 %scatter_fusion = f32[2,2,16384]{1,0,2:T(2,128)} fusion(f32[2,2,16384]{1,0,2:T(2,128)} %broadcast.134.clone, s32[2048]{0:T(1024)S(1)} %get-tuple-element.45, f32[2048,2,2]{2,1,0:T(2,128)S(1)} %copy.624), kind=kCustom, calls=%fused_computation.6 | custom fusion | bytes 106496 | tf_op jit(solution)/shard_map/scatter | solution.py:85
  201.6 19.3 fusion.792
  263.6 93.6 %scatter_fusion.1 = f32[2,2,16,16384]{2,1,3,0:T(2,128)} fusion(f32[2,2,16,16384]{2,1,3,0:T(2,128)} %broadcast.131.clone, s32[1024]{0:T(1024)S(1)} %get-tuple-element.47, f32[1024,2,2,16]{3,2,1,0:T(2,128)S(1)} %copy.634), kind=kCustom, calls=%fused_computation.7 | custom fusion | bytes 790528 | tf_op jit(solution)/shard_map/scatter | solution.py:93
  357.2 23.1 fusion.788
  482.9 36.1 %copy.653 = f32[2,2,16,16384]{2,1,3,0:T(2,128)} copy(f32[2,2,16,16384]{3,2,1,0:T(8,128)} %pad_maximum_fusion.1) | data formatting | bytes 8388608 | tf_op jit(solution)/shard_map/stack | solution.py:26
  519.0 17.8 gather_fusion
  621.9 186.4 %scatter_fusion.2 = f32[2,2,16384]{1,0,2:T(2,128)} fusion(f32[2,2,16384]{1,0,2:T(2,128)} %broadcast.134.clone.1, s32[2048]{0:T(1024)S(1)} %get-tuple-element.45, f32[2048,2,2]{2,1,0:T(2,128)S(1)} %copy.663), kind=kCustom, calls=%fused_computation.8 | custom fusion | bytes 106496 | tf_op jit(solution)/shard_map/scatter | solution.py:85
  808.3 19.3 fusion.791
  879.4 93.6 %scatter_fusion.3 = f32[2,2,16,16384]{2,1,3,0:T(2,128)} fusion(f32[2,2,16,16384]{2,1,3,0:T(2,128)} %broadcast.131.clone.1, s32[1024]{0:T(1024)S(1)} %get-tuple-element.47, f32[1024,2,2,16]{3,2,1,0:T(2,128)S(1)} %copy.673), kind=kCustom, calls=%fused_computation.9 | custom fusion | bytes 790528 | tf_op jit(solution)/shard_map/scatter | solution.py:93
  972.9 23.1 fusion.787
  1098.3 36.1 %copy.692 = f32[2,2,16,16384]{2,1,3,0:T(2,128)} copy(f32[2,2,16,16384]{3,2,1,0:T(8,128)} %pad_maximum_fusion.2) | data formatting | bytes 8388608 | tf_op jit(solution)/shard_map/stack | solution.py:26
  1134.5 17.8 gather_fusion.2
  1252.1 186.4 %scatter_fusion.4 = f32[2,2,16384]{1,0,2:T(2,128)} fusion(f32[2,2,16384]{1,0,2:T(2,128)} %broadcast.134.clone.2, s32[2048]{0:T(1024)S(1)} %get-tuple-element.45, f32[2048,2,2]{2,1,0:T(2,128)S(1)} %copy.703), kind=kCustom, calls=%fused_computation.10 | custom fusion | bytes 106496 | tf_op jit(solution)/shard_map/scatter | solution.py:85
  1438.5 19.3 fusion.790
  1476.3 17.4 all-reduce
  1509.7 93.6 %scatter_fusion.5 = f32[2,2,16,16384]{2,1,3,0:T(2,128)} fusion(f32[2,2,16,16384]{2,1,3,0:T(2,128)} %broadcast.131.clone.2, s32[1024]{0:T(1024)S(1)} %get-tuple-element.47, f32[1024,2,2,16]{3,2,1,0:T(2,128)S(1)} %copy.713), kind=kCustom, calls=%fused_computation.11 | custom fusion | bytes 790528 | tf_op jit(solution)/shard_map/scatter | solution.py:93
  1603.3 23.1 fusion.786
  1728.7 36.1 %copy.732 = f32[2,2,16,16384]{2,1,3,0:T(2,128)} copy(f32[2,2,16,16384]{3,2,1,0:T(8,128)} %pad_maximum_fusion.3) | data formatting | bytes 8388608 | tf_op jit(solution)/shard_map/stack | solution.py:26
  1764.8 17.8 gather_fusion.4
  1863.7 186.4 %scatter_fusion.6 = f32[2,2,16384]{1,0,2:T(2,128)} fusion(f32[2,2,16384]{1,0,2:T(2,128)} %broadcast.134, s32[2048]{0:T(1024)S(1)} %get-tuple-element.45, f32[2048,2,2]{2,1,0:T(2,128)S(1)} %copy.742), kind=kCustom, calls=%fused_computation.12 | custom fusion | bytes 106496 | tf_op jit(solution)/shard_map/scatter | solution.py:85
  2050.1 19.3 fusion.789
  2106.8 93.6 %scatter_fusion.7 = f32[2,2,16,16384]{2,1,3,0:T(2,128)} fusion(f32[2,2,16,16384]{2,1,3,0:T(2,128)} %broadcast.131, s32[1024]{0:T(1024)S(1)} %get-tuple-element.47, f32[1024,2,2,16]{3,2,1,0:T(2,128)S(1)} %copy.752), kind=kCustom, calls=%fused_computation.13 | custom fusion | bytes 790528 | tf_op jit(solution)/shard_map/scatter | solution.py:93
  2200.4 23.1 fusion.785
  2283.1 26.8 %reduce-scatter.2.cloned.1.call-done = f32[16,32,128]{2,1,0:T(8,128)} async-done(((f32[16,128,128]{2,1,0:T(8,128)}), f32[16,32,128]{2,1,0:T(8,128)}) %reduce-scatter.2.cloned.1.call-update) | async-done | bytes 262160 | tf_op jit(solution)/shard_map/reduce_scatter | solution.py:165
  (344 shorter events, 805.8 us)
Async XLA Ops:
  231.9 9.6 copy-start.27
  231.9 9.6 copy-start.23
  233.0 8.6 copy-start.29
  233.0 8.8 copy-start.24
  234.5 16.7 all-to-all-start
  393.5 4.9 copy-start.2
  433.6 4.0 copy-start.10
  542.1 7.4 copy-start.28
  542.1 7.4 copy-start.30
  545.7 13.3 all-to-all-start.1
  582.7 13.6 copy-start.1
  582.7 31.0 %copy-start = (f32[2,64,2048]{2,1,0:T(8,128)S(1)}, f32[2,64,2048]{2,1,0:T(8,128)}, u32[]{:S(2)}) copy-start(f32[2,64,2048]{2,1,0:T(8,128)} %param.20) | copy-start | bytes 3145732
  838.6 24.8 %copy-start.31 = (f32[64]{0:T(128)S(1)}, f32[64]{0:T(128)}, u32[]{:S(2)}) copy-start(f32[64]{0:T(128)} %param.22) | copy-start | bytes 772
  838.6 24.8 %copy-start.32 = (f32[64]{0:T(128)S(1)}, f32[64]{0:T(128)}, u32[]{:S(2)}) copy-start(f32[64]{0:T(128)} %param.21) | copy-start | bytes 772
  841.1 23.8 %all-to-all-start.2 = ((f32[2,2,128,128]{3,1,0,2:T(2,128)}), f32[2,2,128,128]{3,1,0,2:T(2,128)S(1)}, u32[]{:S(2)}, u32[]{:S(2)}) async-start(f32[2,2,128,128]{3,1,0,2:T(2,128)} %copy.670), calls=%async_computation.2 | async-start | bytes 524288 | tf_op jit(solution)/shard_map/all_to_all | solution.py:116
  1009.2 4.9 copy-start.4
  1038.4 4.0 copy-start.17
  1161.1 13.2 all-to-all-start.3
  1471.3 23.9 %all-to-all-start.4 = ((f32[2,2,128,128]{3,1,0,2:T(2,128)}), f32[2,2,128,128]{3,1,0,2:T(2,128)S(1)}, u32[]{:S(2)}, u32[]{:S(2)}) async-start(f32[2,2,128,128]{3,1,0,2:T(2,128)} %copy.710), calls=%async_computation.4 | async-start | bytes 524288 | tf_op jit(solution)/shard_map/all_to_all | solution.py:116
  1639.6 4.9 copy-start.6
  1791.4 13.1 all-to-all-start.5
  1794.9 515.0 %reduce-scatter.2.cloned.1.call-start = ((), (), s32[]{:S(2)}) async-start(), calls=%async_computation.8 | async-start | bytes 1310720 | tf_op jit(solution)/shard_map/reduce_scatter | solution.py:165
  1856.6 7.1 copy-start.25
  2236.7 4.9 copy-start.8
  (16 other events, 53.6 us)
Sparse Core Ops, SparseCore 0:
  2283.2 26.6 reduce-scatter.1
where the time goes:
time: 2350 us; the launch traced here: 2320 us
  local copies, waits for them, and re-layouts  1820 us (77%)
  matrix products  254 us (11%)
  blocking collectives  105 us (4%)
  waiting for transfers between devices  61.5 us (3%)
  other arithmetic  39.9 us (2%)
  starting transfers between devices  24.9 us (1%)
    scatter x4, local copies, waits for them, and re-layouts, to_sticks(): flat_grid = jnp.zeros((2, item_count, grid_size * columns), jnp.float32)....  746 us
    scatter x4, local copies, waits for them, and re-layouts, planes_inverse(): flat_grid = flat_grid.at[:, :, :, stick_pos].set(received)  374 us
    dot_general x84, matrix products, product(): return jnp.einsum(einsum_form, table, operand, precision=PRECISE)  241 us
    slice x11, local copies, waits for them, and re-layouts, complex_transform(): real_part, imag_part = (values_in[0], values_in[1])  170 us
    squeeze x16, local copies, waits for them, and re-layouts, complex_transform(): real_part, imag_part = (values_in[0], values_in[1])  148 us
    another operation x19, local copies, waits for them, and re-layouts, complex_transform(): jnp.stack([product(cosine_table, real_part) - direction_sign * product(si...  128 us
    another operation x9, local copies, waits for them, and re-layouts  68.1 us
    gather x3, local copies, waits for them, and re-layouts, planes_forward(): return jnp.take(spectrum, stick_pos, axis=3)  53.4 us
  transfers between devices with their start and end apart: 7, of which 5 were waited for; matrix products, arithmetic and copies ran while one was open for 0% of the time, Pallas kernels for 0%

commit v1 on v0

--- a/solution.py
+++ b/solution.py
@@ -117,7 +117,12 @@
         )
 
     def from_sticks(back_values):
-        sticks = lax.all_to_all(back_values, "pw", split_axis=3, concat_axis=2, tiled=True)
+        sticks = jnp.concatenate(
+            lax.all_to_all(
+                jnp.stack(jnp.split(back_values, lax.axis_size("pw"), axis=3)), "pw", 0, 0
+            ),
+            2,
+        )
         item_count = sticks.shape[1]
         spectrum = complex_transform(sticks, tables, -1.0, "zk,bks->bzs") * norm_scale
         spectrum = spectrum.reshape(2, item_count, grid_size * columns)

time: 2350 us -> 2320 us (0.987)
    another operation x9 -> x39, local copies, waits for them, and re-layouts: 68.1 us -> 76.1 us
where the time goes in v1:
time: 2320 us; the launch traced here: 2290 us
  local copies, waits for them, and re-layouts  1800 us (78%)
  matrix products  254 us (11%)
  blocking collectives  104 us (4%)
  waiting for transfers between devices  61.7 us (3%)
  other arithmetic  30.8 us (1%)
  starting transfers between devices  23.8 us (1%)
    scatter x4, local copies, waits for them, and re-layouts, to_sticks(): flat_grid = jnp.zeros((2, item_count, grid_size * columns), jnp.float32)....  748 us
    scatter x4, local copies, waits for them, and re-layouts, planes_inverse(): flat_grid = flat_grid.at[:, :, :, stick_pos].set(received)  375 us
    dot_general x84, matrix products, product(): return jnp.einsum(einsum_form, table, operand, precision=PRECISE)  241 us
    slice x11, local copies, waits for them, and re-layouts, complex_transform(): real_part, imag_part = (values_in[0], values_in[1])  170 us
    squeeze x16, local copies, waits for them, and re-layouts, complex_transform(): real_part, imag_part = (values_in[0], values_in[1])  148 us
    another operation x19, local copies, waits for them, and re-layouts, complex_transform(): jnp.stack([product(cosine_table, real_part) - direction_sign * product(si...  129 us
    another operation x9, local copies, waits for them, and re-layouts  68.2 us
    psum x3, blocking collectives, projections(): lax.psum((project_onto(psi, vector), project_onto(beta, vector)), 'pw')  49.3 us
  transfers between devices with their start and end apart: 7, of which 5 were waited for; matrix products, arithmetic and copies ran while one was open for 0% of the time, Pallas kernels for 0%

profile of v1, /device:TPU:0, one launch (start us, length us, event | category | flops | bytes accessed | tf_op | source)
XLA Modules:
  0.0 2289.3 jit_solution(778797705320769484)
XLA Ops:
  15.3 186.9 %scatter_fusion = f32[2,2,16384]{1,0,2:T(2,128)} fusion(f32[2,2,16384]{1,0,2:T(2,128)} %broadcast.134.clone, s32[2048]{0:T(1024)S(1)} %get-tuple-element.69, f32[2048,2,2]{2,1,0:T(2,128)S(1)} %copy.681), kind=kCustom, calls=%fused_computation.6 | custom fusion | bytes 106496 | tf_op jit(solution)/shard_map/scatter | solution.py:85
  202.2 19.3 fusion.792
  263.1 93.7 %scatter_fusion.1 = f32[2,2,16,16384]{2,1,3,0:T(2,128)} fusion(f32[2,2,16,16384]{2,1,3,0:T(2,128)} %broadcast.131.clone, s32[1024]{0:T(1024)S(1)} %get-tuple-element.71, f32[1024,2,2,16]{3,2,1,0:T(2,128)S(1)} %copy.691), kind=kCustom, calls=%fused_computation.7 | custom fusion | bytes 790528 | tf_op jit(solution)/shard_map/scatter | solution.py:93
  356.8 23.1 %fusion.788 = (f32[1,2,16,16384]{2,1,3,0:T(2,128)}, f32[1,2,16,16384]{2,1,3,0:T(2,128)}) fusion(f32[2,2,16,16384]{2,1,3,0:T(2,128)} %scatter_fusion.1), kind=kLoop, calls=%fused_computation.890 | loop fusion | bytes 8388608 | tf_op jit(solution)/shard_map/slice | solution.py:21
  482.6 36.2 %copy.710 = f32[2,2,16,16384]{2,1,3,0:T(2,128)} copy(f32[2,2,16,16384]{3,2,1,0:T(8,128)} %pad_maximum_fusion.1) | data formatting | bytes 8388608 | tf_op jit(solution)/shard_map/stack | solution.py:26
  559.0 14.8 copy.726
  612.6 186.9 %scatter_fusion.2 = f32[2,2,16384]{1,0,2:T(2,128)} fusion(f32[2,2,16384]{1,0,2:T(2,128)} %broadcast.134.clone.1, s32[2048]{0:T(1024)S(1)} %get-tuple-element.69, f32[2048,2,2]{2,1,0:T(2,128)S(1)} %copy.728), kind=kCustom, calls=%fused_computation.8 | custom fusion | bytes 106496 | tf_op jit(solution)/shard_map/scatter | solution.py:85
  799.5 19.3 fusion.791
  837.4 17.3 all-reduce.2
  870.6 93.7 %scatter_fusion.3 = f32[2,2,16,16384]{2,1,3,0:T(2,128)} fusion(f32[2,2,16,16384]{2,1,3,0:T(2,128)} %broadcast.131.clone.1, s32[1024]{0:T(1024)S(1)} %get-tuple-element.71, f32[1024,2,2,16]{3,2,1,0:T(2,128)S(1)} %copy.738), kind=kCustom, calls=%fused_computation.9 | custom fusion | bytes 790528 | tf_op jit(solution)/shard_map/scatter | solution.py:93
  964.3 23.1 %fusion.787 = (f32[1,2,16,16384]{2,1,3,0:T(2,128)}, f32[1,2,16,16384]{2,1,3,0:T(2,128)}) fusion(f32[2,2,16,16384]{2,1,3,0:T(2,128)} %scatter_fusion.3), kind=kLoop, calls=%fused_computation.889 | loop fusion | bytes 8388608 | tf_op jit(solution)/shard_map/slice | solution.py:21
  1089.6 36.2 %copy.757 = f32[2,2,16,16384]{2,1,3,0:T(2,128)} copy(f32[2,2,16,16384]{3,2,1,0:T(8,128)} %pad_maximum_fusion.2) | data formatting | bytes 8388608 | tf_op jit(solution)/shard_map/stack | solution.py:26
  1165.6 14.8 copy.773
  1231.3 186.9 %scatter_fusion.4 = f32[2,2,16384]{1,0,2:T(2,128)} fusion(f32[2,2,16384]{1,0,2:T(2,128)} %broadcast.134.clone.2, s32[2048]{0:T(1024)S(1)} %get-tuple-element.69, f32[2048,2,2]{2,1,0:T(2,128)S(1)} %copy.776), kind=kCustom, calls=%fused_computation.10 | custom fusion | bytes 106496 | tf_op jit(solution)/shard_map/scatter | solution.py:85
  1418.2 19.3 fusion.790
  1456.1 17.5 all-reduce
  1489.6 93.7 %scatter_fusion.5 = f32[2,2,16,16384]{2,1,3,0:T(2,128)} fusion(f32[2,2,16,16384]{2,1,3,0:T(2,128)} %broadcast.131.clone.2, s32[1024]{0:T(1024)S(1)} %get-tuple-element.71, f32[1024,2,2,16]{3,2,1,0:T(2,128)S(1)} %copy.786), kind=kCustom, calls=%fused_computation.11 | custom fusion | bytes 790528 | tf_op jit(solution)/shard_map/scatter | solution.py:93
  1583.3 23.1 %fusion.786 = (f32[1,2,16,16384]{2,1,3,0:T(2,128)}, f32[1,2,16,16384]{2,1,3,0:T(2,128)}) fusion(f32[2,2,16,16384]{2,1,3,0:T(2,128)} %scatter_fusion.5), kind=kLoop, calls=%fused_computation.888 | loop fusion | bytes 8388608 | tf_op jit(solution)/shard_map/slice | solution.py:21
  1708.3 36.2 %copy.805 = f32[2,2,16,16384]{2,1,3,0:T(2,128)} copy(f32[2,2,16,16384]{3,2,1,0:T(8,128)} %pad_maximum_fusion.3) | data formatting | bytes 8388608 | tf_op jit(solution)/shard_map/stack | solution.py:26
  1835.0 186.9 %scatter_fusion.6 = f32[2,2,16384]{1,0,2:T(2,128)} fusion(f32[2,2,16384]{1,0,2:T(2,128)} %broadcast.134, s32[2048]{0:T(1024)S(1)} %get-tuple-element.69, f32[2048,2,2]{2,1,0:T(2,128)S(1)} %copy.823), kind=kCustom, calls=%fused_computation.12 | custom fusion | bytes 106496 | tf_op jit(solution)/shard_map/scatter | solution.py:85
  2022.0 19.3 fusion.789
  2078.7 93.7 %scatter_fusion.7 = f32[2,2,16,16384]{2,1,3,0:T(2,128)} fusion(f32[2,2,16,16384]{2,1,3,0:T(2,128)} %broadcast.131, s32[1024]{0:T(1024)S(1)} %get-tuple-element.71, f32[1024,2,2,16]{3,2,1,0:T(2,128)S(1)} %copy.833), kind=kCustom, calls=%fused_computation.13 | custom fusion | bytes 790528 | tf_op jit(solution)/shard_map/scatter | solution.py:93
  2172.4 23.1 %fusion.785 = (f32[1,2,16,16384]{2,1,3,0:T(2,128)}, f32[1,2,16,16384]{2,1,3,0:T(2,128)}) fusion(f32[2,2,16,16384]{2,1,3,0:T(2,128)} %scatter_fusion.7), kind=kLoop, calls=%fused_computation.887 | loop fusion | bytes 8388608 | tf_op jit(solution)/shard_map/slice | solution.py:21
  2255.4 26.8 %reduce-scatter.2.cloned.1.call-done = f32[16,32,128]{2,1,0:T(8,128)} async-done(((f32[16,128,128]{2,1,0:T(8,128)}), f32[16,32,128]{2,1,0:T(8,128)}) %reduce-scatter.2.cloned.1.call-update) | async-done | bytes 262160 | tf_op jit(solution)/shard_map/reduce_scatter | solution.py:170
  (385 shorter events, 781.5 us)
Async XLA Ops:
  232.5 8.5 copy-start.27
  232.5 8.5 copy-start.23
  233.6 7.5 copy-start.29
  233.6 7.7 copy-start.24
  235.1 15.6 all-to-all-start
  393.1 4.9 copy-start.2
  433.2 4.0 copy-start.10
  536.4 10.2 copy-start.28
  536.4 10.2 copy-start.30
  542.6 13.5 all-to-all-start.1
  573.8 13.6 copy-start.1
  573.8 30.6 %copy-start = (f32[2,64,2048]{2,1,0:T(8,128)S(1)}, f32[2,64,2048]{2,1,0:T(8,128)}, u32[]{:S(2)}) copy-start(f32[2,64,2048]{2,1,0:T(8,128)} %param.20) | copy-start | bytes 3145732
  829.8 24.8 %copy-start.31 = (f32[64]{0:T(128)S(1)}, f32[64]{0:T(128)}, u32[]{:S(2)}) copy-start(f32[64]{0:T(128)} %param.22) | copy-start | bytes 772
  829.8 24.8 %copy-start.32 = (f32[64]{0:T(128)S(1)}, f32[64]{0:T(128)}, u32[]{:S(2)}) copy-start(f32[64]{0:T(128)} %param.21) | copy-start | bytes 772
  832.3 23.8 %all-to-all-start.2 = ((f32[2,2,128,128]{3,1,0,2:T(2,128)}), f32[2,2,128,128]{3,1,0,2:T(2,128)S(1)}, u32[]{:S(2)}, u32[]{:S(2)}) async-start(f32[2,2,128,128]{3,1,0,2:T(2,128)} %copy.735), calls=%async_computation.2 | async-start | bytes 524288 | tf_op jit(solution)/shard_map/all_to_all | solution.py:116
  1000.6 5.0 copy-start.4
  1029.6 4.0 copy-start.17
  1149.5 13.2 all-to-all-start.3
  1451.1 24.1 %all-to-all-start.4 = ((f32[2,2,128,128]{3,1,0,2:T(2,128)}), f32[2,2,128,128]{3,1,0,2:T(2,128)S(1)}, u32[]{:S(2)}, u32[]{:S(2)}) async-start(f32[2,2,128,128]{3,1,0,2:T(2,128)} %copy.783), calls=%async_computation.4 | async-start | bytes 524288 | tf_op jit(solution)/shard_map/all_to_all | solution.py:116
  1619.6 5.0 copy-start.6
  1768.3 13.1 all-to-all-start.5
  1771.7 510.5 %reduce-scatter.2.cloned.1.call-start = ((), (), s32[]{:S(2)}) async-start(), calls=%async_computation.8 | async-start | bytes 1310720 | tf_op jit(solution)/shard_map/reduce_scatter | solution.py:170
  1827.9 7.1 copy-start.25
  2208.7 5.0 copy-start.8
  (16 other events, 53.5 us)
Sparse Core Ops, SparseCore 0:
  2255.5 26.6 reduce-scatter.1
